TPU v7x, 512 devices: a whole 4x8x8 slice. The times are simulated.
512 devices in a mesh: row: 64 (over y_lo, z, core), col: 8 (over y_hi, x).
Axes of the slice: x: 4, y: 8 (y_hi: 2, y_lo: 4; y = y_hi * 4 + y_lo), z: 8, core: 2. Of those that a mesh axis runs over, the one named last changes fastest.
Arguments:
- vectors: float32 [32768, 1024], P('row', 'col'), may hold values from -6 to 6
- householder: float32 [2, 32768, 256], P(None, 'row', 'col'), may hold values from -0.03125 to 0.03125
- tfactors: float32 [2, 256, 256], P(None, None, 'col'), may hold values from -0.17 to 2, as said below
Outputs:
- transformed: float32 [32768, 1024], P('row', 'col')
Inputs may be any that keep to these rules, and one draw needn't show every extreme that they name: Each tfactors[b] is upper triangular with a positive diagonal between 1 and 2.
All inputs are finite; a program needn't handle non-finite values.
Results may differ from a plain program's by a relative error of at most 0.0001.
Values sent between devices are 32-bit elements; how exact they have to be, the bound alone decides.
A program may use at most 64 MiB of HBM per device.

v0:
```python
import jax
import jax.numpy as jnp
from jax import lax
from jax.sharding import PartitionSpec as P

BLOCKS = 2


def turned_gather(arrays, axis, dims):
    turned = [jnp.moveaxis(a, dim, 0) for a, dim in zip(arrays, dims)]
    both = jnp.concatenate([t.reshape(len(t), -1) for t in turned], axis=1)
    whole, at, finished = (lax.all_gather(both, axis, axis=0, tiled=True), 0, [])
    for t, dim in zip(turned, dims):
        section = whole[:, at : at + t[0].size].reshape(-1, *t.shape[1:])
        finished.append(jnp.moveaxis(section, 0, dim))
        at += t[0].size
    return tuple(finished)


def split_up(value, dim, length):
    before, after = (value.shape[:dim], value.shape[dim + 1 :])
    return jnp.moveaxis(value.reshape(*before, length, -1, *after), dim, 0)


def summed_on_arrival(value, axis, dim):
    length = lax.axis_size(axis)
    tiles = lax.all_to_all(split_up(value, dim, length), axis, 0, 0, tiled=True)
    return jnp.sum(tiles, axis=0)


def joined_along(tiles, dim):
    lengths = list(tiles.shape[1:])
    lengths[dim] *= tiles.shape[0]
    return jnp.moveaxis(tiles, 0, dim).reshape(lengths)


def copy_for_each(value, axis):
    copies = jnp.broadcast_to(value, (lax.axis_size(axis), *value.shape))
    return lax.all_to_all(copies, axis, split_axis=0, concat_axis=0, tiled=True)


def collect(value, axis, dim):
    return joined_along(copy_for_each(value, axis), dim)


def project(current, blockv):
    return lax.dot_general(
        current,
        blockv,
        (((0,), (0,)), ((), ())),
        precision=lax.Precision.HIGHEST,
        preferred_element_type=jnp.float32,
    )


def apply_factor(products_t, blockt):
    return lax.dot_general(
        products_t,
        blockt,
        (((1,), (1,)), ((), ())),
        precision=lax.Precision.HIGHEST,
        preferred_element_type=jnp.float32,
    )


def on_device(vectors, householder, tfactors):
    current = vectors
    for block in range(BLOCKS):
        blockv, blockt = turned_gather((householder[block], tfactors[block]), "col", (1, 1))
        source = current
        shares = summed_on_arrival(project(source, blockv), "row", 0)
        reflect_share = apply_factor(shares, blockt)
        reflect_t = collect(reflect_share, "row", 0)
        current = current - lax.dot_general(
            blockv,
            reflect_t,
            (((1,), (1,)), ((), ())),
            precision=lax.Precision.HIGHEST,
            preferred_element_type=jnp.float32,
        )
    return current


def solution(mesh):
    return jax.shard_map(
        on_device,
        mesh=mesh,
        in_specs=(P("row", "col"), P(None, "row", "col"), P(None, None, "col")),
        out_specs=P("row", "col"),
        check_vma=False,
    )
```

profile of v0, /device:TPU:1, one launch (start us, length us, event | category | flops | bytes accessed | tf_op | source)
XLA Modules:
  0.0 163.8 jit_solution(3380706604660088206)
XLA Ops:
  0.0 0.8 slice_bitcast_fusion.2
  0.8 0.1 copy-done.1
  1.0 0.0 copy-start
  1.0 45.1 %all_gather.6 = f32[256,768]{1,0:T(8,128)S(1)} all-gather(f32[32,768]{1,0:T(8,128)S(1)} %pad_maximum_fusion), channel_id=1, replica_groups=mesh['row'=64,'col'=8] {'col'}, dimensions={0}, use_global_device_ids=true | all-gather | bytes 884736 | tf_op jit(solution)/shard_map/all_gather | solution.py:12
  46.1 0.6 convolution_bitcast_fusion
  46.7 0.7 reshape.12
  47.5 15.6 %all-to-all-start = ((f32[64,2,256]{2,1,0:T(2,128)}), f32[64,2,256]{2,1,0:T(2,128)S(1)}, u32[]{:S(2)}, u32[]{:S(2)}) async-start(f32[64,2,256]{2,1,0:T(2,128)} %reshape.12), calls=%async_computation | async-start | bytes 262144 | tf_op jit(solution)/shard_map/all_to_all | solution.py:27
  63.1 10.0 %all-to-all-done = f32[64,2,256]{2,1,0:T(2,128)S(1)} async-done(((f32[64,2,256]{2,1,0:T(2,128)}), f32[64,2,256]{2,1,0:T(2,128)S(1)}, u32[]{:S(2)}, u32[]{:S(2)}) %all-to-all-start) | async-done | bytes 131104 | tf_op jit(solution)/shard_map/all_to_all | solution.py:27
  73.0 0.1 reduce_sum.18
  73.1 0.2 fusion.7
  73.3 0.7 broadcast_in_dim.6
  74.0 5.0 %all-to-all-start.1 = ((f32[64,2,256]{2,1,0:T(2,128)}), f32[64,2,256]{2,1,0:T(2,128)S(1)}, u32[]{:S(2)}, u32[]{:S(2)}) async-start(f32[64,2,256]{2,1,0:T(2,128)} %broadcast_in_dim.6), calls=%async_computation.1 | async-start | bytes 262144 | tf_op jit(solution)/shard_map/all_to_all | solution.py:39
  79.0 40.2 %all_gather.7 = f32[256,768]{1,0:T(8,128)S(1)} all-gather(f32[32,768]{1,0:T(8,128)S(1)} %pad_maximum_fusion.1), channel_id=1, replica_groups=mesh['row'=64,'col'=8] {'col'}, dimensions={0}, use_global_device_ids=true | all-gather | bytes 884736 | tf_op jit(solution)/shard_map/all_gather | solution.py:12
  119.2 0.1 reshape.13
  119.3 1.0 convolution_subtract_fusion.1
  120.3 0.6 fusion.1
  120.9 0.1 reshape.14
  121.0 26.1 %all_to_all.20 = f32[64,2,256]{2,1,0:T(2,128)S(1)} all-to-all(f32[64,2,256]{2,1,0:T(2,128)S(1)} %reshape.14), channel_id=1, replica_groups=mesh['row'=64,'col'=8] {'row'}, dimensions={0} | all-to-all | bytes 262144 | tf_op jit(solution)/shard_map/all_to_all | solution.py:27
  147.1 0.1 reduce_sum.19
  147.1 0.2 fusion.5
  147.3 0.1 broadcast_in_dim.7
  147.4 14.6 %all_to_all.21 = f32[64,2,256]{2,1,0:T(2,128)S(1)} all-to-all(f32[64,2,256]{2,1,0:T(2,128)S(1)} %broadcast_in_dim.7), channel_id=1, replica_groups=mesh['row'=64,'col'=8] {'row'}, dimensions={0} | all-to-all | bytes 262144 | tf_op jit(solution)/shard_map/all_to_all | solution.py:39
  162.0 0.1 reshape.15
  162.1 1.7 %convolution_subtract_fusion = f32[512,128]{1,0:T(8,128)} fusion(f32[512,128]{1,0:T(8,128)S(1)} %convolution_subtract_fusion.1, f32[128,256]{1,0:T(8,128)S(1)} %reshape.15, f32[256,768]{1,0:T(8,128)S(1)} %all_gather.7), kind=kOutput, calls=%fused_computation | convolution fusion | flops 201392128 | bytes 1179648 | tf_op jit(solution)/shard_map/dot_general | solution.py:74
  (6 shorter events, 0.0 us)
Async XLA Ops:
  0.0 0.9 copy-start.1
  1.0 45.2 %copy-start = (f32[512,128]{1,0:T(8,128)S(1)}, f32[512,128]{1,0:T(8,128)}, u32[]{:S(2)}) copy-start(f32[512,128]{1,0:T(8,128)} %param.3) | copy-start | bytes 786436
  47.5 25.6 %all-to-all-start = ((f32[64,2,256]{2,1,0:T(2,128)}), f32[64,2,256]{2,1,0:T(2,128)S(1)}, u32[]{:S(2)}, u32[]{:S(2)}) async-start(f32[64,2,256]{2,1,0:T(2,128)} %reshape.12), calls=%async_computation | async-start | bytes 262144 | tf_op jit(solution)/shard_map/all_to_all | solution.py:27
  74.0 45.2 %all-to-all-start.1 = ((f32[64,2,256]{2,1,0:T(2,128)}), f32[64,2,256]{2,1,0:T(2,128)S(1)}, u32[]{:S(2)}, u32[]{:S(2)}) async-start(f32[64,2,256]{2,1,0:T(2,128)} %broadcast_in_dim.6), calls=%async_computation.1 | async-start | bytes 262144 | tf_op jit(solution)/shard_map/all_to_all | solution.py:39
where the time goes:
time: 164 us
  blocking collectives  126 us (77%)
  starting transfers between devices  20.6 us (13%)
  waiting for transfers between devices  9.97 us (6%)
  matrix products  4.25 us (3%)
  local copies, waits for them, and re-layouts  2.75 us (2%)
    all_gather x2, blocking collectives, turned_gather(): lax.all_gather(both, axis, axis=0, tiled=True)  85.3 us
    all_to_all x1, blocking collectives, summed_on_arrival(): tiles = lax.all_to_all(split_up(value, dim, length), axis, 0, 0, tiled=True)  26.1 us
    all_to_all x1, starting transfers between devices, summed_on_arrival(): tiles = lax.all_to_all(split_up(value, dim, length), axis, 0, 0, tiled=True)  15.6 us
    all_to_all x1, blocking collectives, copy_for_each(): return lax.all_to_all(copies, axis, split_axis=0, concat_axis=0, tiled=True)  14.6 us
    all_to_all x1, waiting for transfers between devices, summed_on_arrival(): tiles = lax.all_to_all(split_up(value, dim, length), axis, 0, 0, tiled=True)  9.97 us
    all_to_all x1, starting transfers between devices, copy_for_each(): return lax.all_to_all(copies, axis, split_axis=0, concat_axis=0, tiled=True)  4.96 us
  transfers between devices with their start and end apart: 2, of which 1 were waited for; matrix products, arithmetic and copies ran while one was open for 0% of the time, Pallas kernels for 0%

commit v1 on v0

--- a/solution.py
+++ b/solution.py
@@ -9,7 +9,13 @@
 def turned_gather(arrays, axis, dims):
     turned = [jnp.moveaxis(a, dim, 0) for a, dim in zip(arrays, dims)]
     both = jnp.concatenate([t.reshape(len(t), -1) for t in turned], axis=1)
-    whole, at, finished = (lax.all_gather(both, axis, axis=0, tiled=True), 0, [])
+    whole, at, finished = (
+        jnp.concatenate(
+            lax.all_to_all(jnp.stack([both] * lax.axis_size(axis)), axis, 0, 0), axis=0
+        ),
+        0,
+        [],
+    )
     for t, dim in zip(turned, dims):
         section = whole[:, at : at + t[0].size].reshape(-1, *t.shape[1:])
         finished.append(jnp.moveaxis(section, 0, dim))

time: 164 us -> 136 us (0.83)
  blocking collectives: 126 us -> 95.3 us
  waiting for transfers between devices: 9.97 us -> 23.9 us
  starting transfers between devices: 20.6 us -> 8.51 us
    all_gather x2 -> x0, blocking collectives: 85.3 us -> none  [turned_gather(): lax.all_gather(both, axis, axis=0, tiled=True)]
    all_to_all x1 -> x2, blocking collectives: 26.1 us -> 53.5 us  [summed_on_arrival(): tiles = lax.all_to_all(split_up(value, dim, length), axis, 0, 0, tiled=True)]
    all_to_all x0 -> x1, blocking collectives: none -> 27.2 us  [turned_gather(): lax.all_to_all(jnp.stack([both] * lax.axis_size(axis)), axis, 0, 0)]
    all_to_all x1, starting transfers between devices: 15.6 us -> 3.55 us  [turned_gather(): lax.all_to_all(jnp.stack([both] * lax.axis_size(axis)), axis, 0, 0)]
    all_to_all x1, waiting for transfers between devices: 0.01 us -> 10.1 us  [copy_for_each(): return lax.all_to_all(copies, axis, split_axis=0, concat_axis=0, tiled=True)]
    all_to_all x1, waiting for transfers between devices: 9.97 us -> 13.8 us  [turned_gather(): lax.all_to_all(jnp.stack([both] * lax.axis_size(axis)), axis, 0, 0)]
  transfers between devices with their start and end apart: 2 -> 2, of which waited for: 1 -> 2; matrix products, arithmetic and copies ran while one was open for 0% -> 1% of each run, Pallas kernels for 0% -> 0%
where the time goes in v1:
time: 136 us; the launch traced here: 135 us
  blocking collectives  95.3 us (70%)
  waiting for transfers between devices  23.9 us (18%)
  starting transfers between devices  8.51 us (6%)
  matrix products  4.24 us (3%)
  local copies, waits for them, and re-layouts  3.11 us (2%)
    all_to_all x2, blocking collectives, summed_on_arrival(): tiles = lax.all_to_all(split_up(value, dim, length), axis, 0, 0, tiled=True)  53.5 us
    all_to_all x1, blocking collectives, turned_gather(): lax.all_to_all(jnp.stack([both] * lax.axis_size(axis)), axis, 0, 0)  27.2 us
    all_to_all x1, blocking collectives, copy_for_each(): return lax.all_to_all(copies, axis, split_axis=0, concat_axis=0, tiled=True)  14.6 us
    all_to_all x1, waiting for transfers between devices, turned_gather(): lax.all_to_all(jnp.stack([both] * lax.axis_size(axis)), axis, 0, 0)  13.8 us
    all_to_all x1, waiting for transfers between devices, copy_for_each(): return lax.all_to_all(copies, axis, split_axis=0, concat_axis=0, tiled=True)  10.1 us
    all_to_all x1, starting transfers between devices, copy_for_each(): return lax.all_to_all(copies, axis, split_axis=0, concat_axis=0, tiled=True)  4.96 us
    all_to_all x1, starting transfers between devices, turned_gather(): lax.all_to_all(jnp.stack([both] * lax.axis_size(axis)), axis, 0, 0)  3.55 us
  transfers between devices with their start and end apart: 2, of which 2 were waited for; matrix products, arithmetic and copies ran while one was open for 1% of the time, Pallas kernels for 0%

profile of v1, /device:TPU:1, one launch (start us, length us, event | category | flops | bytes accessed | tf_op | source)
XLA Modules:
  0.0 135.3 jit_solution(13194665184520119837)
XLA Ops:
  0.0 0.8 slice_bitcast_fusion.2
  0.8 0.1 copy-done.1
  1.0 27.2 %all_to_all.30 = f32[8,32,768]{2,1,0:T(8,128)S(1)} all-to-all(f32[8,32,768]{2,1,0:T(8,128)S(1)} %stack.4), channel_id=1, replica_groups=mesh['row'=64,'col'=8] {'col'}, dimensions={0} | all-to-all | bytes 1572864 | tf_op jit(solution)/shard_map/all_to_all | solution.py:14
  28.3 0.6 convolution_bitcast_fusion
  28.9 0.1 reshape.23
  28.9 29.8 %all_to_all.31 = f32[64,2,256]{2,1,0:T(2,128)S(1)} all-to-all(f32[64,2,256]{2,1,0:T(2,128)S(1)} %reshape.23), channel_id=1, replica_groups=mesh['row'=64,'col'=8] {'row'}, dimensions={0} | all-to-all | bytes 262144 | tf_op jit(solution)/shard_map/all_to_all | solution.py:33
  58.8 0.1 reduce_sum.18
  58.9 0.2 fusion.7
  59.0 0.7 broadcast_in_dim.6
  59.8 5.0 %all-to-all-start.2 = ((f32[64,2,256]{2,1,0:T(2,128)}), f32[64,2,256]{2,1,0:T(2,128)S(1)}, u32[]{:S(2)}, u32[]{:S(2)}) async-start(f32[64,2,256]{2,1,0:T(2,128)} %broadcast_in_dim.6), calls=%async_computation.2 | async-start | bytes 262144 | tf_op jit(solution)/shard_map/all_to_all | solution.py:45
  64.8 10.1 %all-to-all-done.2 = f32[64,2,256]{2,1,0:T(2,128)S(1)} async-done(((f32[64,2,256]{2,1,0:T(2,128)}), f32[64,2,256]{2,1,0:T(2,128)S(1)}, u32[]{:S(2)}, u32[]{:S(2)}) %all-to-all-start.2) | async-done | bytes 131104 | tf_op jit(solution)/shard_map/all_to_all | solution.py:45
  74.9 1.0 stack.5
  75.8 3.5 %all-to-all-start.3 = ((f32[8,32,768]{2,1,0:T(8,128)}), f32[8,32,768]{2,1,0:T(8,128)S(1)}, u32[]{:S(2)}, u32[]{:S(2)}) async-start(f32[8,32,768]{2,1,0:T(8,128)} %stack.5), calls=%async_computation.3 | async-start | bytes 1572864 | tf_op jit(solution)/shard_map/all_to_all | solution.py:14
  79.4 0.1 reshape.24
  79.5 1.0 convolution_subtract_fusion.1
  80.5 13.8 %all-to-all-done.3 = f32[8,32,768]{2,1,0:T(8,128)S(1)} async-done(((f32[8,32,768]{2,1,0:T(8,128)}), f32[8,32,768]{2,1,0:T(8,128)S(1)}, u32[]{:S(2)}, u32[]{:S(2)}) %all-to-all-start.3) | async-done | bytes 786464 | tf_op jit(solution)/shard_map/all_to_all | solution.py:14
  94.2 0.6 fusion.1
  94.9 23.6 %all_to_all.32 = f32[64,2,256]{2,1,0:T(2,128)S(1)} all-to-all(f32[64,2,256]{2,1,0:T(2,128)S(1)} %reshape.26), channel_id=1, replica_groups=mesh['row'=64,'col'=8] {'row'}, dimensions={0} | all-to-all | bytes 262144 | tf_op jit(solution)/shard_map/all_to_all | solution.py:33
  118.5 0.1 reduce_sum.19
  118.6 0.2 fusion.5
  118.8 0.1 broadcast_in_dim.7
  118.9 14.6 %all_to_all.33 = f32[64,2,256]{2,1,0:T(2,128)S(1)} all-to-all(f32[64,2,256]{2,1,0:T(2,128)S(1)} %broadcast_in_dim.7), channel_id=1, replica_groups=mesh['row'=64,'col'=8] {'row'}, dimensions={0} | all-to-all | bytes 262144 | tf_op jit(solution)/shard_map/all_to_all | solution.py:45
  133.5 0.1 reshape.27
  133.6 1.7 %convolution_subtract_fusion = f32[512,128]{1,0:T(8,128)} fusion(f32[512,128]{1,0:T(8,128)S(1)} %convolution_subtract_fusion.1, f32[128,256]{1,0:T(8,128)S(1)} %reshape.27, f32[256,768]{1,0:T(8,128)S(1)} %bitcast.31), kind=kOutput, calls=%fused_computation | convolution fusion | flops 201392128 | bytes 1179648 | tf_op jit(solution)/shard_map/dot_general | solution.py:80
  (8 shorter events, 0.2 us)
Async XLA Ops:
  0.0 0.9 copy-start.1
  1.0 27.2 %copy-start = (f32[512,128]{1,0:T(8,128)S(1)}, f32[512,128]{1,0:T(8,128)}, u32[]{:S(2)}) copy-start(f32[512,128]{1,0:T(8,128)} %param.3) | copy-start | bytes 786436
  59.8 15.1 %all-to-all-start.2 = ((f32[64,2,256]{2,1,0:T(2,128)}), f32[64,2,256]{2,1,0:T(2,128)S(1)}, u32[]{:S(2)}, u32[]{:S(2)}) async-start(f32[64,2,256]{2,1,0:T(2,128)} %broadcast_in_dim.6), calls=%async_computation.2 | async-start | bytes 262144 | tf_op jit(solution)/shard_map/all_to_all | solution.py:45
  75.8 18.4 %all-to-all-start.3 = ((f32[8,32,768]{2,1,0:T(8,128)}), f32[8,32,768]{2,1,0:T(8,128)S(1)}, u32[]{:S(2)}, u32[]{:S(2)}) async-start(f32[8,32,768]{2,1,0:T(8,128)} %stack.5), calls=%async_computation.3 | async-start | bytes 1572864 | tf_op jit(solution)/shard_map/all_to_all | solution.py:14
